TPU v7x, 128 devices: a whole 4x4x4 slice. The times are simulated.
128 devices in a mesh: grp: 4 (over x_hi, core), tile: 32 (over x_lo, y, z).
Axes of the slice: x: 4 (x_hi: 2, x_lo: 2; x = x_hi * 2 + x_lo), y: 4, z: 4, core: 2. Of those that a mesh axis runs over, the one named last changes fastest.
Arguments:
- start_field: float32 [512, 512, 512], P('grp', 'tile'), may hold values from -4 to 4
- class_ids: int32 [512, 512], P('tile'), may hold values from 0 to 7
- run_levels: int32 [512, 8], replicated, may hold values from 0 to 7
- steepness: float32 [512], replicated, may hold values from 0.1 to 1
- step_pick: int32 [512], replicated, may hold values from 1 to 4
- input_layer: float32 [69, 2048], replicated, may hold values from -2 to 2
- output_layer: bfloat16 [2048, 262144], P(None, ('grp', 'tile')), may hold values from -0.125 to 0.125
- output_bias: float32 [262144], P(('grp', 'tile')), may hold values from -1.5 to 1.5
Outputs:
- misfit: bfloat16 [512, 262144], P(None, ('grp', 'tile'))
- output_next: bfloat16 [2048, 262144], P(None, ('grp', 'tile'))
- bias_next: float32 [262144], P(('grp', 'tile'))
- input_next: float32 [69, 2048], replicated
All inputs are finite; a program needn't handle non-finite values.
Results may differ from a plain program's by a relative error of at most 0.0029.
The roundings to bfloat16 on the way count: a program that leaves them out, or rounds other values in their place, can miss the bound.
Values sent between devices are 32-bit elements; how exact they have to be, the bound alone decides.
A program may use at most 128 MiB of HBM per device.

v0:
```python
import jax
import jax.numpy as jnp
from jax import lax
from jax.sharding import Mesh
from jax.sharding import PartitionSpec as P

STEPS = 4
LEVELS = 8
GRP = ("grp_0", "grp_1")
GRP_TILE = ("grp_0", "grp_1", "tile")


def with_halo(value, sides, width):
    for axis, dim in sides:
        size, length = (lax.axis_size(axis), value.shape[dim])
        up = [(i, (i + 1) % size) for i in range(size - 1)]
        down = [(j, i) for i, j in up]
        last = lax.slice_in_dim(value, length - width, length, axis=dim)
        initial = lax.slice_in_dim(value, 0, width, axis=dim)
        before = lax.ppermute(last, axis, up)
        after = lax.ppermute(initial, axis, down)
        value = jnp.concatenate([before, value, after], axis=dim)
    return value


def in_blocks(value, dim, length):
    shape = value.shape
    tiles = value.reshape(*shape[:dim], length, shape[dim] // length, *shape[dim + 1 :])
    return jnp.moveaxis(tiles, dim, 0)


def in_order(tiles, dim):
    tiles = jnp.moveaxis(tiles, 0, dim)
    shape = tiles.shape
    return tiles.reshape(*shape[:dim], shape[dim] * shape[dim + 1], *shape[dim + 2 :])


def turned_blocks(tiles, axes, order):
    inside = tiles.shape[1:]
    out = tiles.reshape(*(lax.axis_size(a) for a in axes), *inside)
    for k in order:
        out = lax.all_to_all(out, axes[k], k, k, tiled=True)
    return out.reshape(-1, *inside)


def core_and_chips(value, groups, order, split_dim, concat_dim):
    length = lax.axis_size(groups[0]) * lax.axis_size(groups[1])
    tiles = in_blocks(value, split_dim, length)
    return in_order(turned_blocks(tiles, groups, order), concat_dim)


def coefficients(run_levels, class_ids):
    table = 0.03 * jnp.exp(run_levels.astype(jnp.float32) * jnp.log(jnp.float32(1.35)))
    kappa = jnp.zeros((run_levels.shape[0],) + class_ids.shape, jnp.float32)
    for klass in range(run_levels.shape[1]):
        picked = jnp.where(class_ids == klass, 1.0, 0.0).astype(jnp.float32)
        kappa = kappa + picked[None] * table[:, klass][:, None, None]
    return kappa


def advance(field, kappa, steep):
    ratio = field * field
    spread = kappa * (1.0 + steep * ratio) / (1.0 + ratio)
    fpad = jnp.pad(field, ((0, 0), (0, 0), (1, 1)))
    spad = jnp.pad(spread, ((0, 0), (0, 0), (1, 1)))
    centre = field[:, 1:-1]
    middle = spread[:, 1:-1]
    total = centre + 0.5 * (middle + spread[:, :-2]) * (field[:, :-2] - centre)
    total = total + 0.5 * (middle + spread[:, 2:]) * (field[:, 2:] - centre)
    total = total + 0.5 * (middle + spad[:, 1:-1, :-2]) * (fpad[:, 1:-1, :-2] - centre)
    total = total + 0.5 * (middle + spad[:, 1:-1, 2:]) * (fpad[:, 1:-1, 2:] - centre)
    return total


def features(run_levels, step_pick, steepness):
    count = run_levels.shape[0]
    onehot = (run_levels[:, :, None] == jnp.arange(LEVELS, dtype=jnp.int32)[None, None, :]).astype(
        jnp.float32
    )
    onehot = onehot.reshape(count, -1)
    moment = (step_pick[:, None] == jnp.arange(1, STEPS + 1, dtype=jnp.int32)[None, :]).astype(
        jnp.float32
    )
    return jnp.concatenate([onehot, moment, steepness[:, None]], axis=1)


def dsilu(pre):
    logistic = jax.nn.sigmoid(pre)
    return logistic * (1.0 + pre * (1.0 - logistic))


def on_device(
    start_field, class_ids, run_levels, steepness, step_pick, input_layer, output_layer, output_bias
):
    local_runs, rows, columns = start_field.shape
    first_run = lax.axis_index(GRP) * local_runs
    levels_here = lax.dynamic_slice_in_dim(run_levels, first_run, local_runs, 0)
    steep = lax.dynamic_slice_in_dim(steepness, first_run, local_runs, 0)[:, None, None]
    pick_here = lax.dynamic_slice_in_dim(step_pick, first_run, local_runs, 0)[:, None, None]
    snapshot = jnp.zeros_like(start_field)
    class_wide = with_halo(class_ids + 1, (("tile", 0),), STEPS)
    kappa_wide = coefficients(levels_here, class_wide - 1)
    wide = with_halo(start_field, (("tile", 1),), STEPS)
    first_row = lax.axis_index("tile") * rows - STEPS
    total_rows = rows * lax.axis_size("tile")
    span = kappa_wide.shape[1]
    for step in range(STEPS):
        margin = STEPS - step - 1
        kappa_now = kappa_wide[:, step : span - step]
        wide = advance(wide, kappa_now, steep)
        row_ids = first_row + step + 1 + jnp.arange(wide.shape[1], dtype=jnp.int32)
        inside = (row_ids >= 0) & (row_ids < total_rows)
        wide = jnp.where(inside[None, :, None], wide, 0.0)
        snapshot = jnp.where(pick_here == step + 1, wide[:, margin : margin + rows], snapshot)
    flat = snapshot.reshape(local_runs, rows * columns)
    target = core_and_chips(flat, ("grp_0", "grp_1"), (0, 1), 1, 0)
    runs_total = target.shape[0]
    feats = features(run_levels, step_pick, steepness)
    pre = jnp.dot(feats, input_layer, precision=lax.Precision.HIGHEST)
    hidden = jax.nn.silu(pre).astype(jnp.bfloat16)
    error = (
        jnp.dot(hidden, output_layer, preferred_element_type=jnp.float32)
        + output_bias[None, :]
        - target
    )
    slope = (error * (2.0 / runs_total)).astype(jnp.bfloat16)
    grad = lax.dot_general(
        hidden, slope, (((0,), (0,)), ((), ())), preferred_element_type=jnp.float32
    )
    output_next = (output_layer.astype(jnp.float32) - 0.5 * grad).astype(jnp.bfloat16)
    bias_next = output_bias - 0.5 * jnp.sum(slope.astype(jnp.float32), axis=0)
    gain_slope = dsilu(pre)
    partial_back = lax.dot_general(
        slope, output_layer, (((1,), (1,)), ((), ())), preferred_element_type=jnp.float32
    )
    partial_in = lax.dot_general(
        feats, partial_back * gain_slope, (((0,), (0,)), ((), ())), precision=lax.Precision.HIGHEST
    )
    grad_in = lax.psum(partial_in, GRP_TILE)
    input_next = input_layer - 2.0 * grad_in
    return (error.astype(jnp.bfloat16), output_next, bias_next, input_next)


def solution(mesh):
    split = Mesh(mesh.devices.reshape(2, 2, mesh.shape["tile"]), ("grp_0", "grp_1", "tile"))
    return jax.shard_map(
        on_device,
        mesh=split,
        in_specs=(
            P(GRP, "tile", None),
            P("tile", None),
            P(),
            P(),
            P(),
            P(),
            P(None, GRP_TILE),
            P(GRP_TILE),
        ),
        out_specs=(P(None, GRP_TILE), P(None, GRP_TILE), P(GRP_TILE), P()),
        check_vma=False,
    )
```

profile of v0, /device:TPU:1, one launch (start us, length us, event | category | flops | bytes accessed | tf_op | source)
XLA Modules:
  0.0 382.8 jit_solution(13823181372475220173)
XLA Ops:
  7.2 0.8 broadcast_add_fusion
  8.0 4.4 %collective-permute-start.2 = (s32[4,512]{1,0:T(4,128)S(1)}, s32[4,512]{1,0:T(4,128)S(1)}, u32[]{:S(2)}, u32[]{:S(2)}) collective-permute-start(s32[4,512]{1,0:T(4,128)S(1)} %get-tuple-element.24), channel_id=1, source_target_pairs={{0,1},{1,2},{2,3},{3,4},{4,5},{5,6},{6,7},{7,8},{8,9},{9,10},{10,1... | collective-permute-start | bytes 24584 | tf_op jit(solution)/shard_map/ppermute | solution.py:20
  12.3 1.3 collective-permute-start.3
  13.6 2.7 fusion.90
  16.7 4.2 %collective-permute-start = (f32[128,4,512]{2,0,1:T(8,128)S(1)}, f32[128,4,512]{2,0,1:T(8,128)S(1)}, u32[]{:S(2)}, u32[]{:S(2)}) collective-permute-start(f32[128,4,512]{2,0,1:T(8,128)S(1)} %copy.34), channel_id=1, source_target_pairs={{0,1},{1,2},{2,3},{3,4},{4,5},{5,6},{6,7},{7,8},{8,9},{9,10},{10,1... | collective-permute-start | bytes 3145736 | tf_op jit(solution)/shard_map/ppermute | solution.py:20
  21.0 1.3 copy.35
  22.3 1.3 collective-permute-start.1
  25.4 1.3 broadcast_compare_fusion.3
  27.8 5.3 %copy.29 = f32[128,16,512]{0,2,1:T(8,128)} copy(f32[128,16,512]{2,1,0:T(8,128)} %param.8) | data formatting | bytes 8388608 | tf_op args[0]
  33.1 0.8 dynamic_slice.11
  34.0 14.8 %multiply_add_fusion = f32[128,24,512]{0,2,1:T(8,128)} fusion(f32[128]{0:T(128)S(1)} %get-tuple-element.27, f32[24,512]{1,0:T(8,128)S(1)} %get-tuple-element.23, f32[128]{0:T(128)S(1)} %get-tuple-element.28, f32[24,512]{1,0:T(8,128)S(1)} %get-tuple-element.22, f32[128]{0:T(128)S(1)} %get-tuple-element.29, f32[24,512]{1,0:T(8,128)S(1)} %get-tuple-element.21, ...), kind=kLoop, calls=%fused_computation.3 | loop fusion | flops 23592960 | bytes 6688768 | tf_op jit(solution)/shard_map/add | solution.py:57
  49.3 1.5 copy.30
  50.9 1.0 copy-done.3
  52.0 2.7 pad_maximum_fusion
  55.4 15.7 %add_divide_fusion = f32[128,24,512]{0,2,1:T(8,128)S(1)} fusion(f32[128]{0:T(128)S(1)} %dynamic_slice.11, f32[128,4,512]{0,2,1:T(8,128)} %copy-done.3, f32[128,16,512]{0,2,1:T(8,128)S(1)} %copy-done.2, f32[128,4,512]{0,2,1:T(8,128)S(1)} %copy.28, f32[128]{0:T(128)S(1)} %copy-done.25, f32[24,512]{1,0:T(8,128)S(1)} %copy-done.9, f32[128]{0:T(128)S(1)} %copy-done.27, ...), kind=kLoop, calls=%fused_computation.2 | loop fusion | flops 36175872 | bytes 12980736 | tf_op jit(solution)/shard_map/div | solution.py:63
  71.1 11.3 %fusion.11 = (f32[128,22,512]{0,2,1:T(8,128)}, f32[128,22,512]{0,2,1:T(8,128)S(1)}) fusion(f32[128,24,512]{0,2,1:T(8,128)} %multiply_add_fusion, f32[128]{0:T(128)S(1)} %dynamic_slice.11, f32[128,24,512]{0,2,1:T(8,128)S(1)} %pad_maximum_fusion, f32[128,24,512]{0,2,1:T(8,128)S(1)} %add_divide_fusion, pred[22]{0:T(512)(128)(4,1)} %compare_and_fusion), kind=kLoop, calls=%fused_computation.20 | loop fusion | flops 38928384 | bytes 64487960 | tf_op jit(solution)/shard_map/div | solution.py:63
  82.4 16.6 %fusion.29 = (f32[128,20,512]{0,2,1:T(8,128)S(1)}, f32[128,20,512]{0,2,1:T(8,128)S(1)}) fusion(f32[128,24,512]{0,2,1:T(8,128)} %multiply_add_fusion, f32[128]{0:T(128)S(1)} %dynamic_slice.11, f32[128,22,512]{0,2,1:T(8,128)S(1)} %get-tuple-element.11, f32[128,22,512]{0,2,1:T(8,128)} %get-tuple-element.10, pred[20]{0:T(512)(128)(4,1)S(1)} %copy-done.46), kind=kLoop, calls=%fused_computation.47 | loop fusion | flops 35389440 | bytes 58721280 | tf_op jit(solution)/shard_map/div | solution.py:63
  99.1 10.9 %fusion.47 = (f32[128,18,512]{0,2,1:T(8,128)}, f32[128,18,512]{0,2,1:T(8,128)}) fusion(f32[128,24,512]{0,2,1:T(8,128)} %multiply_add_fusion, f32[128]{0:T(128)S(1)} %dynamic_slice.11, f32[128,20,512]{0,2,1:T(8,128)S(1)} %get-tuple-element.9, f32[128,20,512]{0,2,1:T(8,128)S(1)} %get-tuple-element.8, pred[18]{0:T(512)(128)(4,1)S(1)} %copy-done.45), kind=kLoop, calls=%fused_computation.74 | loop fusion | flops 31850496 | bytes 52954112 | tf_op jit(solution)/shard_map/div | solution.py:63
  110.0 21.7 %fusion.60 = f32[128,16,512]{0,2,1:T(8,128)} fusion(f32[128,18,512]{0,2,1:T(8,128)} %get-tuple-element.6, f32[128,18,512]{0,2,1:T(8,128)} %get-tuple-element.7, f32[128,22,512]{0,2,1:T(8,128)} %copy-done, f32[128,20,512]{0,2,1:T(8,128)} %copy-done.1, pred[16]{0:T(512)(128)(4,1)S(1)} %copy-done.44, pred[128]{0:T(512)(128)(4,1)S(1)} %copy-done.43, ...), kind=kLoop, calls=%fused_computation.95 | loop fusion | flops 26214400 | bytes 47186448 | tf_op jit(solution)/shard_map/jit(_where)/select_n | solution.py:114
  131.7 5.6 %copy.31 = f32[4,128,2048]{2,1,0:T(8,128)} copy(f32[4,128,2048]{1,2,0:T(8,128)} %bitcast.30) | data formatting | bytes 8388608 | tf_op jit(solution)/shard_map/transpose | solution.py:29
  137.3 5.8 %all-to-all-start = ((f32[2,2,128,2048]{3,2,1,0:T(8,128)}), f32[2,2,128,2048]{3,2,1,0:T(8,128)}, u32[]{:S(2)}, u32[]{:S(2)}) async-start(f32[2,2,128,2048]{3,2,1,0:T(8,128)} %bitcast.31), calls=%async_computation | async-start | bytes 8388608 | tf_op jit(solution)/shard_map/all_to_all | solution.py:42
  143.4 5.1 %fusion.82 = f32[512,2048]{1,0:T(8,128)} fusion(f32[69,2048]{1,0:T(8,128)S(1)} %copy-done.5, f32[512,1]{0,1:T(1,128)S(1)} %bitcast.32, f32[512,4]{0,1:T(4,128)S(1)} %compare_convert_fusion, f32[512,64]{0,1:T(8,128)S(1)} %fusion.81), kind=kOutput, calls=%fused_computation.130 | convolution fusion | flops 868291584 | bytes 4900864 | tf_op jit(solution)/shard_map/dot_general | solution.py:119
  148.5 42.2 %all-to-all-done = f32[2,2,128,2048]{3,2,1,0:T(8,128)} async-done(((f32[2,2,128,2048]{3,2,1,0:T(8,128)}), f32[2,2,128,2048]{3,2,1,0:T(8,128)}, u32[]{:S(2)}, u32[]{:S(2)}) %all-to-all-start) | async-done | bytes 4194336 | tf_op jit(solution)/shard_map/all_to_all | solution.py:42
  190.6 2.6 copy.32
  193.3 9.2 %all_to_all.10 = f32[2,2,128,2048]{3,2,0,1:T(8,128)S(1)} all-to-all(f32[2,2,128,2048]{3,2,0,1:T(8,128)S(1)} %copy.32), channel_id=1, replica_groups=mesh['grp_0'=2,'grp_1'=2,'tile'=32] {'grp_1'}, dimensions={1} | all-to-all | bytes 8388608 | tf_op jit(solution)/shard_map/all_to_all | solution.py:42
  203.0 1.7 copy-done.4
  204.7 6.1 %convert_reduce_fusion = (f32[2048]{0:T(1024)S(1)}, bf16[512,2048]{1,0:T(8,128)(2,1)}, f32[512,2048]{1,0:T(8,128)S(1)}) fusion(f32[2,2,128,2048]{3,2,1,0:T(8,128)S(1)} %copy.33, f32[2048]{0:T(1024)S(1)} %copy-done.23, bf16[2048,2048]{1,0:T(8,128)(2,1)S(1)} %bitcast.35, f32[512,2048]{1,0:T(8,128)S(1)} %copy-done.4), kind=kOutput, calls=%fused_computation.121 | convolution fusion | flops 4307548160 | bytes 23085056 | tf_op jit(solution)/shard_map/dot_general | solution.py:122
  210.8 6.1 %fusion.86 = f32[512,2048]{1,0:T(8,128)} fusion(bf16[2048,2048]{1,0:T(8,128)(2,1)S(1)} %bitcast.35, f32[512,2048]{1,0:T(8,128)S(1)} %get-tuple-element.37), kind=kOutput, calls=%fused_computation.164 | convolution fusion | flops 4297064448 | bytes 16777216 | tf_op jit(solution)/shard_map/dot_general | solution.py:133
  216.8 7.0 %fusion.74 = f32[69,2048]{1,0:T(8,128)} fusion(f32[512,2048]{1,0:T(8,128)} %fusion.86, f32[512,2048]{1,0:T(8,128)S(1)} %copy-done.4, f32[512,1]{0,1:T(1,128)S(1)} %bitcast.33, f32[512,4]{0,1:T(4,128)S(1)} %compare_convert_fusion, f32[512,64]{0,1:T(8,128)S(1)} %fusion.81), kind=kOutput, calls=%fused_computation.115 | convolution fusion | flops 876680192 | bytes 9095168 | tf_op jit(solution)/shard_map/dot_general | solution.py:136
  223.9 14.6 %subtract_convert_fusion = bf16[2048,2048]{1,0:T(8,128)(2,1)} fusion(bf16[2048,2048]{1,0:T(8,128)(2,1)} %param.14, f32[512,2048]{1,0:T(8,128)} %copy-done.47, f32[512,2048]{1,0:T(8,128)} %fusion.82), kind=kOutput, calls=%fused_computation | convolution fusion | flops 4319084544 | bytes 25165824 | tf_op jit(solution)/shard_map/dot_general | solution.py:127
  239.1 135.0 %all-reduce.10.cloned.1.call-done = f32[69,2048]{1,0:T(8,128)} async-done(((f32[69,2048]{1,0:T(8,128)}), f32[69,2048]{1,0:T(8,128)}) %all-reduce.10.cloned.1.call-update) | async-done | bytes 565264 | tf_op jit(solution)/shard_map/psum | solution.py:139
  374.0 1.9 multiply_subtract_fusion
  (124 shorter events, 5.8 us)
Async XLA Ops:
  7.2 16.4 %copy-start.22 = (s32[512,8]{0,1:T(8,128)S(1)}, s32[512,8]{0,1:T(8,128)}, u32[]{:S(2)}) copy-start(s32[512,8]{0,1:T(8,128)} %param.10) | copy-start | bytes 49156
  8.0 25.9 %collective-permute-start.2 = (s32[4,512]{1,0:T(4,128)S(1)}, s32[4,512]{1,0:T(4,128)S(1)}, u32[]{:S(2)}, u32[]{:S(2)}) collective-permute-start(s32[4,512]{1,0:T(4,128)S(1)} %get-tuple-element.24), channel_id=1, source_target_pairs={{0,1},{1,2},{2,3},{3,4},{4,5},{5,6},{6,7},{7,8},{8,9},{9,10},{10,1... | collective-permute-start | bytes 24584 | tf_op jit(solution)/shard_map/ppermute | solution.py:20
  12.3 21.6 %collective-permute-start.3 = (s32[4,512]{1,0:T(4,128)S(1)}, s32[4,512]{1,0:T(4,128)S(1)}, u32[]{:S(2)}, u32[]{:S(2)}) collective-permute-start(s32[4,512]{1,0:T(4,128)S(1)} %get-tuple-element.25), channel_id=1, source_target_pairs={{1,0},{2,1},{3,2},{4,3},{5,4},{6,5},{7,6},{8,7},{9,8},{10,9},{11,1... | collective-permute-start | bytes 24584 | tf_op jit(solution)/shard_map/ppermute | solution.py:21
  16.7 32.2 %collective-permute-start = (f32[128,4,512]{2,0,1:T(8,128)S(1)}, f32[128,4,512]{2,0,1:T(8,128)S(1)}, u32[]{:S(2)}, u32[]{:S(2)}) collective-permute-start(f32[128,4,512]{2,0,1:T(8,128)S(1)} %copy.34), channel_id=1, source_target_pairs={{0,1},{1,2},{2,3},{3,4},{4,5},{5,6},{6,7},{7,8},{8,9},{9,10},{10,1... | collective-permute-start | bytes 3145736 | tf_op jit(solution)/shard_map/ppermute | solution.py:20
  22.3 27.0 %collective-permute-start.1 = (f32[128,4,512]{2,0,1:T(8,128)}, f32[128,4,512]{2,0,1:T(8,128)}, u32[]{:S(2)}, u32[]{:S(2)}) collective-permute-start(f32[128,4,512]{2,0,1:T(8,128)} %copy.35), channel_id=1, source_target_pairs={{1,0},{2,1},{3,2},{4,3},{5,4},{6,5},{7,6},{8,7},{9,8},{10,9},{11,1... | collective-permute-start | bytes 3145736 | tf_op jit(solution)/shard_map/ppermute | solution.py:21
  23.6 25.2 %copy-start.24 = (f32[128]{0:T(128)}, f32[128]{0:T(128)S(1)}, u32[]{:S(2)}) copy-start(f32[128]{0:T(128)S(1)} %get-tuple-element.27) | copy-start | bytes 1540
  23.6 25.2 %copy-start.26 = (f32[128]{0:T(128)}, f32[128]{0:T(128)S(1)}, u32[]{:S(2)}) copy-start(f32[128]{0:T(128)S(1)} %get-tuple-element.28) | copy-start | bytes 1540
  23.6 25.2 %copy-start.28 = (f32[128]{0:T(128)}, f32[128]{0:T(128)S(1)}, u32[]{:S(2)}) copy-start(f32[128]{0:T(128)S(1)} %get-tuple-element.29) | copy-start | bytes 1540
  23.6 25.2 %copy-start.30 = (f32[128]{0:T(128)}, f32[128]{0:T(128)S(1)}, u32[]{:S(2)}) copy-start(f32[128]{0:T(128)S(1)} %get-tuple-element.30) | copy-start | bytes 1540
  23.6 25.2 %copy-start.32 = (f32[128]{0:T(128)}, f32[128]{0:T(128)S(1)}, u32[]{:S(2)}) copy-start(f32[128]{0:T(128)S(1)} %get-tuple-element.31) | copy-start | bytes 1540
  23.7 25.2 %copy-start.34 = (f32[128]{0:T(128)}, f32[128]{0:T(128)S(1)}, u32[]{:S(2)}) copy-start(f32[128]{0:T(128)S(1)} %get-tuple-element.32) | copy-start | bytes 1540
  23.7 25.2 %copy-start.36 = (f32[128]{0:T(128)}, f32[128]{0:T(128)S(1)}, u32[]{:S(2)}) copy-start(f32[128]{0:T(128)S(1)} %get-tuple-element.33) | copy-start | bytes 1540
  33.9 15.0 %copy-start.6 = (f32[24,512]{1,0:T(8,128)}, f32[24,512]{1,0:T(8,128)S(1)}, u32[]{:S(2)}) copy-start(f32[24,512]{1,0:T(8,128)S(1)} %get-tuple-element.22) | copy-start | bytes 147460
  33.9 15.0 %copy-start.8 = (f32[24,512]{1,0:T(8,128)}, f32[24,512]{1,0:T(8,128)S(1)}, u32[]{:S(2)}) copy-start(f32[24,512]{1,0:T(8,128)S(1)} %get-tuple-element.23) | copy-start | bytes 147460
  34.0 14.9 %copy-start.10 = (f32[24,512]{1,0:T(8,128)}, f32[24,512]{1,0:T(8,128)S(1)}, u32[]{:S(2)}) copy-start(f32[24,512]{1,0:T(8,128)S(1)} %get-tuple-element.16) | copy-start | bytes 147460
  34.0 14.9 %copy-start.12 = (f32[24,512]{1,0:T(8,128)}, f32[24,512]{1,0:T(8,128)S(1)}, u32[]{:S(2)}) copy-start(f32[24,512]{1,0:T(8,128)S(1)} %get-tuple-element.17) | copy-start | bytes 147460
  34.0 14.9 %copy-start.14 = (f32[24,512]{1,0:T(8,128)}, f32[24,512]{1,0:T(8,128)S(1)}, u32[]{:S(2)}) copy-start(f32[24,512]{1,0:T(8,128)S(1)} %get-tuple-element.18) | copy-start | bytes 147460
  34.0 14.9 %copy-start.16 = (f32[24,512]{1,0:T(8,128)}, f32[24,512]{1,0:T(8,128)S(1)}, u32[]{:S(2)}) copy-start(f32[24,512]{1,0:T(8,128)S(1)} %get-tuple-element.19) | copy-start | bytes 147460
  34.0 14.9 %copy-start.18 = (f32[24,512]{1,0:T(8,128)}, f32[24,512]{1,0:T(8,128)S(1)}, u32[]{:S(2)}) copy-start(f32[24,512]{1,0:T(8,128)S(1)} %get-tuple-element.20) | copy-start | bytes 147460
  34.0 14.9 %copy-start.20 = (f32[24,512]{1,0:T(8,128)}, f32[24,512]{1,0:T(8,128)S(1)}, u32[]{:S(2)}) copy-start(f32[24,512]{1,0:T(8,128)S(1)} %get-tuple-element.21) | copy-start | bytes 147460
  71.1 11.3 %copy-start.46 = (pred[20]{0:T(512)(128)(4,1)S(1)}, pred[20]{0:T(512)(128)(4,1)}, u32[]{:S(2)}) copy-start(pred[20]{0:T(512)(128)(4,1)} %compare_and_fusion.1) | copy-start | bytes 64
  82.4 16.6 %copy-start = (f32[128,22,512]{0,2,1:T(8,128)}, f32[128,22,512]{0,2,1:T(8,128)S(1)}, u32[]{:S(2)}) copy-start(f32[128,22,512]{0,2,1:T(8,128)S(1)} %get-tuple-element.11) | copy-start | bytes 17301508
  82.4 16.7 %copy-start.45 = (pred[18]{0:T(512)(128)(4,1)S(1)}, pred[18]{0:T(512)(128)(4,1)}, u32[]{:S(2)}) copy-start(pred[18]{0:T(512)(128)(4,1)} %compare_and_fusion.2) | copy-start | bytes 58
  99.0 10.9 %copy-start.1 = (f32[128,20,512]{0,2,1:T(8,128)}, f32[128,20,512]{0,2,1:T(8,128)S(1)}, u32[]{:S(2)}) copy-start(f32[128,20,512]{0,2,1:T(8,128)S(1)} %get-tuple-element.9) | copy-start | bytes 15728644
  99.0 10.9 %copy-start.40 = (pred[128]{0:T(512)(128)(4,1)S(1)}, pred[128]{0:T(512)(128)(4,1)}, u32[]{:S(2)}) copy-start(pred[128]{0:T(512)(128)(4,1)} %get-tuple-element.4) | copy-start | bytes 388
  99.0 10.9 %copy-start.41 = (pred[128]{0:T(512)(128)(4,1)S(1)}, pred[128]{0:T(512)(128)(4,1)}, u32[]{:S(2)}) copy-start(pred[128]{0:T(512)(128)(4,1)} %get-tuple-element.34) | copy-start | bytes 388
  99.0 10.9 %copy-start.42 = (pred[128]{0:T(512)(128)(4,1)S(1)}, pred[128]{0:T(512)(128)(4,1)}, u32[]{:S(2)}) copy-start(pred[128]{0:T(512)(128)(4,1)} %get-tuple-element.35) | copy-start | bytes 388
  99.1 10.9 %copy-start.43 = (pred[128]{0:T(512)(128)(4,1)S(1)}, pred[128]{0:T(512)(128)(4,1)}, u32[]{:S(2)}) copy-start(pred[128]{0:T(512)(128)(4,1)} %get-tuple-element.36) | copy-start | bytes 388
  99.1 10.9 %copy-start.44 = (pred[16]{0:T(512)(128)(4,1)S(1)}, pred[16]{0:T(512)(128)(4,1)}, u32[]{:S(2)}) copy-start(pred[16]{0:T(512)(128)(4,1)} %compare_and_fusion.3) | copy-start | bytes 52
  137.3 53.4 %all-to-all-start = ((f32[2,2,128,2048]{3,2,1,0:T(8,128)}), f32[2,2,128,2048]{3,2,1,0:T(8,128)}, u32[]{:S(2)}, u32[]{:S(2)}) async-start(f32[2,2,128,2048]{3,2,1,0:T(8,128)} %bitcast.31), calls=%async_computation | async-start | bytes 8388608 | tf_op jit(solution)/shard_map/all_to_all | solution.py:42
  143.0 231.0 %all-reduce.10.cloned.1.call-start = ((), (), s32[]{:S(2)}) async-start(), calls=%async_computation.2 | async-start | bytes 1179648 | tf_op jit(solution)/shard_map/psum | solution.py:139
  190.6 12.4 %slice-start = ((s8[8388608]{0:T(1024)(128)(4,1)}), s8[4194304]{0:T(1024)(128)(4,1)S(1)}, s32[]{:S(2)}) async-start(s8[8388608]{0:T(1024)(128)(4,1)} %bitcast.34), calls=%async_computation.3 | async-start | bytes 8388608
  (24 other events, 94.4 us)
Sparse Core Ops, SparseCore 0:
  224.0 150.0 all-reduce.9
where the time goes:
time: 384 us; the launch traced here: 383 us
  waiting for transfers between devices  177 us (46%)
  other arithmetic  101 us (26%)
  matrix products  38.8 us (10%)
  local copies, waits for them, and re-layouts  24.5 us (6%)
  starting transfers between devices  17 us (4%)
  between operations  14.8 us (4%)
  blocking collectives  9.24 us (2%)
    psum x1, waiting for transfers between devices, on_device(): grad_in = lax.psum(partial_in, GRP_TILE)  135 us
    div x4, other arithmetic, advance(): spread = kappa * (1.0 + steep * ratio) / (1.0 + ratio)  54.4 us
    all_to_all x1, waiting for transfers between devices, turned_blocks(): out = lax.all_to_all(out, axes[k], k, k, tiled=True)  42.2 us
    select_n x1, other arithmetic, on_device(): jnp.where(pick_here == step + 1, wide[:, margin:margin + rows], snapshot)  21.7 us
    add x1, other arithmetic, coefficients(): kappa = kappa + picked[None] * table[:, klass][:, None, None]  14.8 us
    dot_general x1, matrix products, on_device(): lax.dot_general(hidden, slope, (((0,), (0,)), ((), ())), preferred_elemen...  14.6 us
    unnamed x103, local copies, waits for them, and re-layouts  10.4 us
    all_to_all x1, blocking collectives, turned_blocks(): out = lax.all_to_all(out, axes[k], k, k, tiled=True)  9.24 us
  transfers between devices with their start and end apart: 6, of which 2 were waited for; matrix products, arithmetic and copies ran while one was open for 13% of the time, Pallas kernels for 0%

commit v1 on v0

--- a/solution.py
+++ b/solution.py
@@ -136,7 +136,7 @@
     partial_in = lax.dot_general(
         feats, partial_back * gain_slope, (((0,), (0,)), ((), ())), precision=lax.Precision.HIGHEST
     )
-    grad_in = lax.psum(partial_in, GRP_TILE)
+    grad_in = jnp.sum(lax.all_gather(partial_in, GRP_TILE), axis=0)
     input_next = input_layer - 2.0 * grad_in
     return (error.astype(jnp.bfloat16), output_next, bias_next, input_next)
 

time: 384 us -> 677 us (1.76)
  waiting for transfers between devices: 177 us -> 448 us
  other arithmetic: 101 us -> 123 us
    all_gather x0 -> x1, waiting for transfers between devices: none -> 406 us  [on_device(): grad_in = jnp.sum(lax.all_gather(partial_in, GRP_TILE), axis=0)]
    psum x1 -> x0, waiting for transfers between devices: 135 us -> none  [on_device(): grad_in = lax.psum(partial_in, GRP_TILE)]
    reduce_sum x0 -> x1, other arithmetic: none -> 23.3 us  [on_device(): grad_in = jnp.sum(lax.all_gather(partial_in, GRP_TILE), axis=0)]
  transfers between devices with their start and end apart: 6 -> 6, of which waited for: 2 -> 2; matrix products, arithmetic and copies ran while one was open for 13% -> 7% of each run, Pallas kernels for 0% -> 0%
where the time goes in v1:
time: 677 us; the launch traced here: 676 us
  waiting for transfers between devices  448 us (66%)
  other arithmetic  123 us (18%)
  matrix products  38.9 us (6%)
  local copies, waits for them, and re-layouts  24.4 us (4%)
  starting transfers between devices  18.5 us (3%)
  between operations  14.8 us (2%)
  blocking collectives  9.24 us (1%)
    all_gather x1, waiting for transfers between devices, on_device(): grad_in = jnp.sum(lax.all_gather(partial_in, GRP_TILE), axis=0)  406 us
    div x4, other arithmetic, advance(): spread = kappa * (1.0 + steep * ratio) / (1.0 + ratio)  53.4 us
    all_to_all x1, waiting for transfers between devices, turned_blocks(): out = lax.all_to_all(out, axes[k], k, k, tiled=True)  42.1 us
    reduce_sum x1, other arithmetic, on_device(): grad_in = jnp.sum(lax.all_gather(partial_in, GRP_TILE), axis=0)  23.3 us
    select_n x1, other arithmetic, on_device(): jnp.where(pick_here == step + 1, wide[:, margin:margin + rows], snapshot)  21.9 us
    add x1, other arithmetic, coefficients(): kappa = kappa + picked[None] * table[:, klass][:, None, None]  14.8 us
    dot_general x1, matrix products, on_device(): lax.dot_general(hidden, slope, (((0,), (0,)), ((), ())), preferred_elemen...  14.6 us
  transfers between devices with their start and end apart: 6, of which 2 were waited for; matrix products, arithmetic and copies ran while one was open for 7% of the time, Pallas kernels for 0%

profile of v1, /device:TPU:1, one launch (start us, length us, event | category | flops | bytes accessed | tf_op | source)
XLA Modules:
  0.0 676.3 jit_solution(16900371005721694945)
XLA Ops:
  7.2 0.8 broadcast_add_fusion
  8.0 4.4 collective-permute-start.2
  12.3 1.3 collective-permute-start.3
  13.6 2.7 fusion.93
  16.7 1.3 collective-permute-start.1
  18.0 1.3 copy.34
  19.3 5.8 collective-permute-start
  26.8 1.3 broadcast_compare_fusion.3
  29.4 5.3 copy.29
  35.6 14.8 %multiply_add_fusion = f32[128,24,512]{0,2,1:T(8,128)} fusion(f32[128]{0:T(128)S(1)} %get-tuple-element.27, f32[24,512]{1,0:T(8,128)S(1)} %get-tuple-element.23, f32[128]{0:T(128)S(1)} %get-tuple-element.28, f32[24,512]{1,0:T(8,128)S(1)} %get-tuple-element.22, f32[128]{0:T(128)S(1)} %get-tuple-element.29, f32[24,512]{1,0:T(8,128)S(1)} %get-tuple-element.21, ...), kind=kLoop, calls=%fused_computation.3 | loop fusion | flops 23592960 | bytes 6688768 | tf_op jit(solution)/shard_map/add | solution.py:57
  50.9 1.5 copy.28
  52.5 1.0 copy-done.3
  53.6 2.8 pad_maximum_fusion
  57.0 14.7 %add_divide_fusion = f32[128,24,512]{0,2,1:T(8,128)S(1)} fusion(f32[128]{0:T(128)S(1)} %dynamic_slice.11, f32[128,4,512]{0,2,1:T(8,128)S(1)} %copy.30, f32[128,16,512]{0,2,1:T(8,128)S(1)} %copy-done.2, f32[128,4,512]{0,2,1:T(8,128)} %copy-done.3, f32[128]{0:T(128)S(1)} %copy-done.25, f32[24,512]{1,0:T(8,128)S(1)} %copy-done.9, f32[128]{0:T(128)S(1)} %copy-done.27, ...), kind=kLoop, calls=%fused_computation.2 | loop fusion | flops 36175872 | bytes 12980736 | tf_op jit(solution)/shard_map/div | solution.py:63
  71.8 11.3 %fusion.11 = (f32[128,22,512]{0,2,1:T(8,128)}, f32[128,22,512]{0,2,1:T(8,128)S(1)}) fusion(f32[128,24,512]{0,2,1:T(8,128)} %multiply_add_fusion, f32[128]{0:T(128)S(1)} %dynamic_slice.11, f32[128,24,512]{0,2,1:T(8,128)S(1)} %pad_maximum_fusion, f32[128,24,512]{0,2,1:T(8,128)S(1)} %add_divide_fusion, pred[22]{0:T(512)(128)(4,1)} %compare_and_fusion), kind=kLoop, calls=%fused_computation.20 | loop fusion | flops 38928384 | bytes 64487960 | tf_op jit(solution)/shard_map/div | solution.py:63
  83.0 16.6 %fusion.29 = (f32[128,20,512]{0,2,1:T(8,128)S(1)}, f32[128,20,512]{0,2,1:T(8,128)S(1)}) fusion(f32[128,24,512]{0,2,1:T(8,128)} %multiply_add_fusion, f32[128]{0:T(128)S(1)} %dynamic_slice.11, f32[128,22,512]{0,2,1:T(8,128)S(1)} %get-tuple-element.11, f32[128,22,512]{0,2,1:T(8,128)} %get-tuple-element.10, pred[20]{0:T(512)(128)(4,1)S(1)} %copy-done.46), kind=kLoop, calls=%fused_computation.47 | loop fusion | flops 35389440 | bytes 58721280 | tf_op jit(solution)/shard_map/div | solution.py:63
  99.7 10.9 %fusion.47 = (f32[128,18,512]{0,2,1:T(8,128)}, f32[128,18,512]{0,2,1:T(8,128)}) fusion(f32[128,24,512]{0,2,1:T(8,128)} %multiply_add_fusion, f32[128]{0:T(128)S(1)} %dynamic_slice.11, f32[128,20,512]{0,2,1:T(8,128)S(1)} %get-tuple-element.9, f32[128,20,512]{0,2,1:T(8,128)S(1)} %get-tuple-element.8, pred[18]{0:T(512)(128)(4,1)S(1)} %copy-done.45), kind=kLoop, calls=%fused_computation.74 | loop fusion | flops 31850496 | bytes 52954112 | tf_op jit(solution)/shard_map/div | solution.py:63
  110.6 21.9 %fusion.60 = f32[128,16,512]{0,2,1:T(8,128)} fusion(f32[128,18,512]{0,2,1:T(8,128)} %get-tuple-element.6, f32[128,18,512]{0,2,1:T(8,128)} %get-tuple-element.7, f32[128,22,512]{0,2,1:T(8,128)} %copy-done, f32[128,20,512]{0,2,1:T(8,128)} %copy-done.1, pred[16]{0:T(512)(128)(4,1)S(1)} %copy-done.44, pred[128]{0:T(512)(128)(4,1)S(1)} %copy-done.43, ...), kind=kLoop, calls=%fused_computation.95 | loop fusion | flops 26214400 | bytes 47186448 | tf_op jit(solution)/shard_map/jit(_where)/select_n | solution.py:114
  132.5 5.5 copy.31
  137.9 5.7 all-to-all-start
  144.0 5.2 fusion.85
  149.2 42.1 %all-to-all-done = f32[2,2,128,2048]{3,2,1,0:T(8,128)} async-done(((f32[2,2,128,2048]{3,2,1,0:T(8,128)}), f32[2,2,128,2048]{3,2,1,0:T(8,128)}, u32[]{:S(2)}, u32[]{:S(2)}) %all-to-all-start) | async-done | bytes 4194336 | tf_op jit(solution)/shard_map/all_to_all | solution.py:42
  191.3 2.6 copy.32
  193.9 9.2 %all_to_all.10 = f32[2,2,128,2048]{3,2,0,1:T(8,128)S(1)} all-to-all(f32[2,2,128,2048]{3,2,0,1:T(8,128)S(1)} %copy.32), channel_id=1, replica_groups=mesh['grp_0'=2,'grp_1'=2,'tile'=32] {'grp_1'}, dimensions={1} | all-to-all | bytes 8388608 | tf_op jit(solution)/shard_map/all_to_all | solution.py:42
  203.7 1.7 copy-done.4
  205.3 6.1 convert_reduce_fusion
  211.4 6.1 fusion.89
  217.5 7.0 %fusion.80 = f32[1,69,2048]{2,1,0:T(8,128)} fusion(f32[512,2048]{1,0:T(8,128)} %fusion.89, f32[512,2048]{1,0:T(8,128)S(1)} %copy-done.4, f32[512,1]{0,1:T(1,128)S(1)} %bitcast.35, f32[512,4]{0,1:T(4,128)S(1)} %compare_convert_fusion, f32[512,64]{0,1:T(8,128)S(1)} %fusion.84), kind=kOutput, calls=%fused_computation.125 | convolution fusion | flops 876680192 | bytes 9095168 | tf_op jit(solution)/shard_map/dot_general | solution.py:136
  225.1 14.6 %subtract_convert_fusion = bf16[2048,2048]{1,0:T(8,128)(2,1)} fusion(bf16[2048,2048]{1,0:T(8,128)(2,1)} %param.14, f32[512,2048]{1,0:T(8,128)} %copy-done.47, f32[512,2048]{1,0:T(8,128)} %fusion.85), kind=kOutput, calls=%fused_computation | convolution fusion | flops 4319084544 | bytes 25165824 | tf_op jit(solution)/shard_map/dot_general | solution.py:127
  239.7 405.5 %all-gather.4.cloned.1.call-done = f32[128,69,2048]{2,1,0:T(8,128)} async-done(((f32[1,69,2048]{2,1,0:T(8,128)}), f32[128,69,2048]{2,1,0:T(8,128)}) %all-gather.4.cloned.1.call-update) | async-done | bytes 72351760 | tf_op jit(solution)/shard_map/all_gather | solution.py:139
  645.2 23.3 %reduce_sum.19 = f32[69,2048]{1,0:T(8,128)S(1)} reduce(f32[128,69,2048]{2,1,0:T(8,128)} %all-gather.4.cloned.1.call-done, f32[]{:T(128)} %constant.40.clone.1), dimensions={0}, to_apply=%region_1.2 | reduce | flops 17946624 | bytes 72916992 | tf_op jit(solution)/shard_map/reduce_sum | solution.py:139
  668.6 0.9 multiply_subtract_fusion
  (125 shorter events, 6.5 us)
Async XLA Ops:
  7.2 21.5 %copy-start.22 = (s32[512,8]{0,1:T(8,128)S(1)}, s32[512,8]{0,1:T(8,128)}, u32[]{:S(2)}) copy-start(s32[512,8]{0,1:T(8,128)} %param.10) | copy-start | bytes 49156
  8.0 27.5 %collective-permute-start.2 = (s32[4,512]{1,0:T(4,128)S(1)}, s32[4,512]{1,0:T(4,128)S(1)}, u32[]{:S(2)}, u32[]{:S(2)}) collective-permute-start(s32[4,512]{1,0:T(4,128)S(1)} %get-tuple-element.24), channel_id=1, source_target_pairs={{0,1},{1,2},{2,3},{3,4},{4,5},{5,6},{6,7},{7,8},{8,9},{9,10},{10,1... | collective-permute-start | bytes 24584 | tf_op jit(solution)/shard_map/ppermute | solution.py:20
  12.3 23.1 %collective-permute-start.3 = (s32[4,512]{1,0:T(4,128)S(1)}, s32[4,512]{1,0:T(4,128)S(1)}, u32[]{:S(2)}, u32[]{:S(2)}) collective-permute-start(s32[4,512]{1,0:T(4,128)S(1)} %get-tuple-element.25), channel_id=1, source_target_pairs={{1,0},{2,1},{3,2},{4,3},{5,4},{6,5},{7,6},{8,7},{9,8},{10,9},{11,1... | collective-permute-start | bytes 24584 | tf_op jit(solution)/shard_map/ppermute | solution.py:21
  16.7 33.8 %collective-permute-start.1 = (f32[128,4,512]{2,0,1:T(8,128)S(1)}, f32[128,4,512]{2,0,1:T(8,128)S(1)}, u32[]{:S(2)}, u32[]{:S(2)}) collective-permute-start(f32[128,4,512]{2,0,1:T(8,128)S(1)} %copy.35), channel_id=1, source_target_pairs={{1,0},{2,1},{3,2},{4,3},{5,4},{6,5},{7,6},{8,7},{9,8},{10,9},{11,1... | collective-permute-start | bytes 3145736 | tf_op jit(solution)/shard_map/ppermute | solution.py:21
  19.3 31.6 %collective-permute-start = (f32[128,4,512]{2,0,1:T(8,128)}, f32[128,4,512]{2,0,1:T(8,128)}, u32[]{:S(2)}, u32[]{:S(2)}) collective-permute-start(f32[128,4,512]{2,0,1:T(8,128)} %copy.34), channel_id=1, source_target_pairs={{0,1},{1,2},{2,3},{3,4},{4,5},{5,6},{6,7},{7,8},{8,9},{9,10},{10,1... | collective-permute-start | bytes 3145736 | tf_op jit(solution)/shard_map/ppermute | solution.py:20
  28.7 21.7 %copy-start.24 = (f32[128]{0:T(128)}, f32[128]{0:T(128)S(1)}, u32[]{:S(2)}) copy-start(f32[128]{0:T(128)S(1)} %get-tuple-element.27) | copy-start | bytes 1540
  28.7 21.7 %copy-start.26 = (f32[128]{0:T(128)}, f32[128]{0:T(128)S(1)}, u32[]{:S(2)}) copy-start(f32[128]{0:T(128)S(1)} %get-tuple-element.28) | copy-start | bytes 1540
  28.7 21.7 %copy-start.28 = (f32[128]{0:T(128)}, f32[128]{0:T(128)S(1)}, u32[]{:S(2)}) copy-start(f32[128]{0:T(128)S(1)} %get-tuple-element.29) | copy-start | bytes 1540
  28.8 21.7 %copy-start.30 = (f32[128]{0:T(128)}, f32[128]{0:T(128)S(1)}, u32[]{:S(2)}) copy-start(f32[128]{0:T(128)S(1)} %get-tuple-element.30) | copy-start | bytes 1540
  28.8 21.7 %copy-start.32 = (f32[128]{0:T(128)}, f32[128]{0:T(128)S(1)}, u32[]{:S(2)}) copy-start(f32[128]{0:T(128)S(1)} %get-tuple-element.31) | copy-start | bytes 1540
  28.8 21.7 %copy-start.34 = (f32[128]{0:T(128)}, f32[128]{0:T(128)S(1)}, u32[]{:S(2)}) copy-start(f32[128]{0:T(128)S(1)} %get-tuple-element.32) | copy-start | bytes 1540
  28.8 21.7 %copy-start.36 = (f32[128]{0:T(128)}, f32[128]{0:T(128)S(1)}, u32[]{:S(2)}) copy-start(f32[128]{0:T(128)S(1)} %get-tuple-element.33) | copy-start | bytes 1540
  35.5 15.0 %copy-start.6 = (f32[24,512]{1,0:T(8,128)}, f32[24,512]{1,0:T(8,128)S(1)}, u32[]{:S(2)}) copy-start(f32[24,512]{1,0:T(8,128)S(1)} %get-tuple-element.22) | copy-start | bytes 147460
  35.5 15.0 %copy-start.8 = (f32[24,512]{1,0:T(8,128)}, f32[24,512]{1,0:T(8,128)S(1)}, u32[]{:S(2)}) copy-start(f32[24,512]{1,0:T(8,128)S(1)} %get-tuple-element.23) | copy-start | bytes 147460
  35.6 14.9 %copy-start.10 = (f32[24,512]{1,0:T(8,128)}, f32[24,512]{1,0:T(8,128)S(1)}, u32[]{:S(2)}) copy-start(f32[24,512]{1,0:T(8,128)S(1)} %get-tuple-element.16) | copy-start | bytes 147460
  35.6 14.9 %copy-start.12 = (f32[24,512]{1,0:T(8,128)}, f32[24,512]{1,0:T(8,128)S(1)}, u32[]{:S(2)}) copy-start(f32[24,512]{1,0:T(8,128)S(1)} %get-tuple-element.17) | copy-start | bytes 147460
  35.6 14.9 %copy-start.14 = (f32[24,512]{1,0:T(8,128)}, f32[24,512]{1,0:T(8,128)S(1)}, u32[]{:S(2)}) copy-start(f32[24,512]{1,0:T(8,128)S(1)} %get-tuple-element.18) | copy-start | bytes 147460
  35.6 14.9 %copy-start.16 = (f32[24,512]{1,0:T(8,128)}, f32[24,512]{1,0:T(8,128)S(1)}, u32[]{:S(2)}) copy-start(f32[24,512]{1,0:T(8,128)S(1)} %get-tuple-element.19) | copy-start | bytes 147460
  35.6 14.9 %copy-start.18 = (f32[24,512]{1,0:T(8,128)}, f32[24,512]{1,0:T(8,128)S(1)}, u32[]{:S(2)}) copy-start(f32[24,512]{1,0:T(8,128)S(1)} %get-tuple-element.20) | copy-start | bytes 147460
  35.6 14.9 %copy-start.20 = (f32[24,512]{1,0:T(8,128)}, f32[24,512]{1,0:T(8,128)S(1)}, u32[]{:S(2)}) copy-start(f32[24,512]{1,0:T(8,128)S(1)} %get-tuple-element.21) | copy-start | bytes 147460
  71.7 11.3 %copy-start.46 = (pred[20]{0:T(512)(128)(4,1)S(1)}, pred[20]{0:T(512)(128)(4,1)}, u32[]{:S(2)}) copy-start(pred[20]{0:T(512)(128)(4,1)} %compare_and_fusion.1) | copy-start | bytes 64
  83.0 16.6 %copy-start = (f32[128,22,512]{0,2,1:T(8,128)}, f32[128,22,512]{0,2,1:T(8,128)S(1)}, u32[]{:S(2)}) copy-start(f32[128,22,512]{0,2,1:T(8,128)S(1)} %get-tuple-element.11) | copy-start | bytes 17301508
  83.0 16.6 %copy-start.45 = (pred[18]{0:T(512)(128)(4,1)S(1)}, pred[18]{0:T(512)(128)(4,1)}, u32[]{:S(2)}) copy-start(pred[18]{0:T(512)(128)(4,1)} %compare_and_fusion.2) | copy-start | bytes 58
  99.6 10.9 %copy-start.1 = (f32[128,20,512]{0,2,1:T(8,128)}, f32[128,20,512]{0,2,1:T(8,128)S(1)}, u32[]{:S(2)}) copy-start(f32[128,20,512]{0,2,1:T(8,128)S(1)} %get-tuple-element.9) | copy-start | bytes 15728644
  99.6 10.9 %copy-start.40 = (pred[128]{0:T(512)(128)(4,1)S(1)}, pred[128]{0:T(512)(128)(4,1)}, u32[]{:S(2)}) copy-start(pred[128]{0:T(512)(128)(4,1)} %get-tuple-element.4) | copy-start | bytes 388
  99.6 10.9 %copy-start.41 = (pred[128]{0:T(512)(128)(4,1)S(1)}, pred[128]{0:T(512)(128)(4,1)}, u32[]{:S(2)}) copy-start(pred[128]{0:T(512)(128)(4,1)} %get-tuple-element.34) | copy-start | bytes 388
  99.6 10.9 %copy-start.42 = (pred[128]{0:T(512)(128)(4,1)S(1)}, pred[128]{0:T(512)(128)(4,1)}, u32[]{:S(2)}) copy-start(pred[128]{0:T(512)(128)(4,1)} %get-tuple-element.35) | copy-start | bytes 388
  99.7 10.9 %copy-start.43 = (pred[128]{0:T(512)(128)(4,1)S(1)}, pred[128]{0:T(512)(128)(4,1)}, u32[]{:S(2)}) copy-start(pred[128]{0:T(512)(128)(4,1)} %get-tuple-element.36) | copy-start | bytes 388
  99.7 10.9 %copy-start.44 = (pred[16]{0:T(512)(128)(4,1)S(1)}, pred[16]{0:T(512)(128)(4,1)}, u32[]{:S(2)}) copy-start(pred[16]{0:T(512)(128)(4,1)} %compare_and_fusion.3) | copy-start | bytes 52
  137.9 53.3 %all-to-all-start = ((f32[2,2,128,2048]{3,2,1,0:T(8,128)}), f32[2,2,128,2048]{3,2,1,0:T(8,128)}, u32[]{:S(2)}, u32[]{:S(2)}) async-start(f32[2,2,128,2048]{3,2,1,0:T(8,128)} %bitcast.33), calls=%async_computation | async-start | bytes 8388608 | tf_op jit(solution)/shard_map/all_to_all | solution.py:42
  143.7 501.5 %all-gather.4.cloned.1.call-start = ((), (), s32[]{:S(2)}) async-start(), calls=%async_computation.2 | async-start | bytes 76087296 | tf_op jit(solution)/shard_map/all_gather | solution.py:139
  191.3 12.4 %slice-start = ((s8[8388608]{0:T(1024)(128)(4,1)}), s8[4194304]{0:T(1024)(128)(4,1)S(1)}, s32[]{:S(2)}) async-start(s8[8388608]{0:T(1024)(128)(4,1)} %bitcast.36), calls=%async_computation.3 | async-start | bytes 8388608
  (24 other events, 94.4 us)
Sparse Core Ops, SparseCore 0:
  224.6 420.5 all-gather.3
